TPU v7x, 512 devices: a whole 4x8x8 slice. The times are simulated.
512 devices in a mesh: sec: 8 (over x, core), xy: 64 (over y, z).
Axes of the slice: x: 4, y: 8, z: 8, core: 2. Of those that a mesh axis runs over, the one named last changes fastest.
Arguments:
- patches: bfloat16 [16, 64, 8, 160, 160], P('sec', 'xy'), may hold values from -100 to 100
- margins: bfloat16 [16, 64, 6, 160, 160], P('sec', 'xy'), may hold values from -100 to 100
- offsets: int32 [16, 64, 8, 2], P('sec', 'xy'), may hold values from -40 to 40
- counts: int32 [16, 64], P('sec', 'xy'), may hold values from 1 to 8
Outputs:
- flow: float32 [16, 64, 2, 8], P('sec', 'xy')
- seams: float32 [16, 64, 2, 6], P('sec', 'xy')
All inputs are finite; a program needn't handle non-finite values.
Results may differ from a plain program's by a relative error of at most 0.022.
The roundings to bfloat16 on the way count: a program that leaves them out, or rounds other values in their place, can miss the bound.
Values may be sent and summed in bfloat16 or wider, within the bound.
A program may use at most 64 MiB of HBM per device.

v0:
```python
import functools

import jax
import jax.numpy as jnp
import ml_dtypes
import numpy as np
from jax import lax
from jax.experimental import pallas as pl
from jax.experimental.pallas import tpu as pltpu
from jax.sharding import PartitionSpec as P

SIDE = 160
HALF = SIDE // 2
PATCH_ROWS = 2
PATCH_COLS = 4
GRID_COLS = 4
SLOTS = PATCH_ROWS * PATCH_COLS
EDGES = PATCH_ROWS + PATCH_COLS
LANES = 128
TAIL = SIDE - LANES
GROUP = 4
BAND = 96
PIXEL_UNIT = 16.0
LOG2E = 1.4426950408889634
SCORE_SCALE = 2.0 / float(SIDE) ** 3
EXP2_SCALE = SCORE_SCALE * LOG2E

T_ROW = 0
WRE_ROW = T_ROW + GROUP * 256
WIM_ROW = WRE_ROW + 256
CS_ROW = WIM_ROW + 256
BACK_ROW = CS_ROW + 2 * BAND
TABLE_ROWS = BACK_ROW + SIDE

NEXT = 16
LEFT = 24
BELOW = 28
IMAGES = 36
PAIRS = 28
PAIR_ROWS = 32

MESH = pl.DeviceIdType.MESH


def tables():
    freq = np.arange(SIDE)
    phase = (freq[:, None] * freq[None, :]) % SIDE
    angle = phase.astype(np.float32) * np.float32(2.0 * np.pi / SIDE)
    cosine = np.cos(angle).astype(ml_dtypes.bfloat16).astype(np.float32)
    sine = np.sin(angle).astype(ml_dtypes.bfloat16).astype(np.float32)
    n = HALF + 1
    out = np.zeros((TABLE_ROWS, 256), np.float32)
    right = np.zeros((SIDE, 256), np.float32)
    right[:, :n] = cosine[:, :n]
    right[:, 128 : 128 + n] = sine[:, :n]
    for p in range(GROUP):
        base = T_ROW + 256 * p
        out[base : base + LANES] = right[:LANES]
        low = base + LANES + TAIL * p
        out[low : low + TAIL] = right[LANES:]
    inner = np.ones((n, 1), np.float32)
    inner[0] = inner[HALF] = 0.0
    cos_half, sin_half = cosine[:n, :n], sine[:n, :n]
    out[WRE_ROW : WRE_ROW + n, :n] = cos_half
    out[WRE_ROW + 128 : WRE_ROW + 128 + n, :n] = cos_half * inner
    out[WRE_ROW : WRE_ROW + n, 128 : 128 + n] = sin_half
    out[WRE_ROW + 128 : WRE_ROW + 128 + n, 128 : 128 + n] = -sin_half * inner
    out[WIM_ROW : WIM_ROW + n, :n] = sin_half
    out[WIM_ROW + 128 : WIM_ROW + 128 + n, :n] = sin_half * inner
    out[WIM_ROW : WIM_ROW + n, 128 : 128 + n] = cos_half
    out[WIM_ROW + 128 : WIM_ROW + 128 + n, 128 : 128 + n] = -cos_half * inner
    out[CS_ROW : CS_ROW + n, :SIDE] = cosine[:n]
    out[CS_ROW + BAND : CS_ROW + BAND + n, :SIDE] = sine[:n]
    twice = 1.0 + inner[:, 0]
    out[BACK_ROW : BACK_ROW + SIDE, :n] = cosine[:, :n] * twice
    out[BACK_ROW : BACK_ROW + SIDE, BAND : BAND + n] = -sine[:, :n] * twice
    return out.astype(ml_dtypes.bfloat16)


def iota(shape, axis):
    return lax.broadcasted_iota(jnp.int32, shape, axis)


def dot(a, b):
    return jnp.dot(a, b, preferred_element_type=jnp.float32)


def wrapped(index, centre):
    return jnp.where(index >= centre + HALF, index - SIDE, index).astype(jnp.float32)


def kernel(
    sections,
    patches,
    margins,
    table_in,
    offsets,
    counts,
    flow_out,
    seams_out,
    table,
    main,
    rem,
    raw,
    spec,
    peak,
    total,
    moment,
    centre,
    mesh_own,
    mesh_in,
    local_sem,
    send_sem,
    recv_sem,
    mesh_send,
    mesh_recv,
):
    sec = lax.axis_index("sec")
    tile = lax.axis_index("xy")
    sec_total = lax.axis_size("sec")
    tile_total = lax.axis_size("xy")
    column = lax.rem(tile, GRID_COLS)
    has_before = sec > 0
    has_after = sec < sec_total - 1
    has_left = column > 0
    has_right = column < GRID_COLS - 1
    has_above = tile >= GRID_COLS
    has_below = tile < tile_total - GRID_COLS

    local_copies = []

    def fetch(src, dst):
        copy = pltpu.make_async_copy(src, dst, local_sem.at[len(local_copies)])
        copy.start()
        local_copies.append(copy)
        return copy

    margin_raw = [
        fetch(margins.at[k, 0, :, :, pl.ds(LANES, TAIL)], raw.at[pl.ds(16 + EDGES * k, EDGES)])
        for k in range(sections)
    ]
    table_copy = fetch(table_in, table)
    patch_raw = [
        fetch(patches.at[k, 0, :, :, pl.ds(LANES, TAIL)], raw.at[pl.ds(SLOTS * k, SLOTS)])
        for k in range(sections)
    ]
    patch_main = [
        fetch(patches.at[k, 0, :, :, pl.ds(0, LANES)], main.at[pl.ds(SLOTS * k, SLOTS)])
        for k in range(sections)
    ]

    barrier = pltpu.get_barrier_semaphore()
    peers = (
        (has_before, (sec - 1, tile)),
        (has_after, (sec + 1, tile)),
        (has_left, (sec, tile - 1)),
        (has_right, (sec, tile + 1)),
        (has_above, (sec, tile - GRID_COLS)),
        (has_below, (sec, tile + GRID_COLS)),
    )
    for there, device in peers:

        @pl.when(there)
        def _(device=device):
            pl.semaphore_signal(barrier, inc=1, device_id=device, device_id_type=MESH)

    def transfer(number, src, dst, device):
        return pltpu.make_async_remote_copy(
            src_ref=src,
            dst_ref=dst,
            send_sem=send_sem.at[number],
            recv_sem=recv_sem.at[number],
            device_id=device,
            device_id_type=MESH,
        )

    before, left, above = (sec - 1, tile), (sec, tile - 1), (sec, tile - GRID_COLS)
    below_main = [
        [
            transfer(
                4 * k + c,
                margins.at[k, 0, PATCH_ROWS + c, :, pl.ds(0, LANES)],
                main.at[BELOW + 4 * k + c],
                above,
            )
            for c in range(PATCH_COLS)
        ]
        for k in range(sections)
    ]
    below_rem = [transfer(8 + k, rem.at[9 + 1 + k], rem.at[7 + k], above) for k in range(sections)]
    left_main = [
        transfer(
            10 + 2 * k + r,
            margins.at[k, 0, r, :, pl.ds(0, LANES)],
            main.at[LEFT + 2 * k + r],
            left,
        )
        for k in range(sections)
        for r in range(PATCH_ROWS)
    ]
    left_rem = transfer(14, rem.at[9], rem.at[6], left)
    next_main = [
        transfer(
            15 + h,
            patches.at[0, 0, pl.ds(4 * h, 4), :, pl.ds(0, LANES)],
            main.at[pl.ds(NEXT + 4 * h, 4)],
            before,
        )
        for h in range(2)
    ]
    next_rem = [transfer(17 + h, rem.at[h], rem.at[4 + h], before) for h in range(2)]

    def start(copies):
        for copy in copies:
            copy.start()

    def pack(slot, sources):
        rem[slot] = jnp.concatenate([raw[i] for i in sources], axis=1)

    table_copy.wait()
    for copy in margin_raw:
        copy.wait()
    pack(10, [16 + PATCH_ROWS + c for c in range(4)])
    pack(11, [16 + EDGES + PATCH_ROWS + c for c in range(4)])
    pack(9, [16, 17, 16 + EDGES, 16 + EDGES + 1])

    greeted = functools.reduce(jnp.add, [there.astype(jnp.int32) for there, _ in peers])
    pl.semaphore_wait(barrier, greeted)

    @pl.when(has_above)
    def _():
        start(below_rem + below_main[0] + below_main[1])

    @pl.when(has_left)
    def _():
        start([left_rem] + left_main)

    @pl.when(has_before)
    def _():
        start(next_main)

    for copy in patch_raw:
        copy.wait()
    for h in range(4):
        pack(h, [4 * h + p for p in range(4)])

    @pl.when(has_before)
    def _():
        start(next_rem)

    for copy in patch_main:
        copy.wait()

    lane = iota((1, LANES), 1)
    group_of_lane = lane // TAIL

    def spectra(group):
        tail = rem[group].astype(jnp.float32)
        tail_sum = jnp.sum(tail, axis=0, keepdims=True)
        means = []
        for p in range(GROUP):
            sums = jnp.sum(main[GROUP * group + p].astype(jnp.float32), axis=0, keepdims=True)
            sums = sums + jnp.where(group_of_lane == p, tail_sum, 0.0)
            means.append(jnp.sum(sums, axis=1, keepdims=True) * (1.0 / (SIDE * SIDE)))

        def by_lane(values):
            out = jnp.broadcast_to(values[0], (1, LANES))
            for p in range(1, GROUP):
                out = jnp.where(group_of_lane == p, values[p], out)
            return out

        tail = tail - by_lane(means)
        tail_sum = jnp.sum(tail * tail, axis=0, keepdims=True)
        scales = []
        for p in range(GROUP):
            centred = main[GROUP * group + p].astype(jnp.float32) - means[p]
            sums = jnp.sum(centred * centred, axis=0, keepdims=True)
            sums = sums + jnp.where(group_of_lane == p, tail_sum, 0.0)
            variance = jnp.sum(sums, axis=1, keepdims=True) * (1.0 / (SIDE * SIDE))
            scales.append(1.0 / jnp.sqrt(variance + 1e-05))
        tail = (tail * by_lane(scales)).astype(jnp.bfloat16)
        for p in range(GROUP):
            image = GROUP * group + p
            head = ((main[image].astype(jnp.float32) - means[p]) * scales[p]).astype(jnp.bfloat16)
            normal = jnp.concatenate([head, tail], axis=1)
            rows = dot(normal, table[T_ROW + 256 * p : T_ROW + 256 * (p + 1)]).astype(jnp.bfloat16)
            both = dot(table[CS_ROW : CS_ROW + 2 * BAND, :SIDE], rows)
            cc, cs = both[:BAND, :LANES], both[:BAND, LANES:]
            sc, ss = both[BAND:, :LANES], both[BAND:, LANES:]
            spec[image, 0] = jnp.concatenate([cc - ss, cc + ss], axis=1).astype(jnp.bfloat16)
            spec[image, 1] = jnp.concatenate([-(sc + cs), sc - cs], axis=1).astype(jnp.bfloat16)

    shift_rows = iota((16, SIDE), 1)
    kind = iota((16, SIDE), 0)

    def displace(pair, source, target, centre_row, centre_col):
        a_re, a_im = spec[source, 0].astype(jnp.float32), spec[source, 1].astype(jnp.float32)
        b_re, b_im = spec[target, 0].astype(jnp.float32), spec[target, 1].astype(jnp.float32)
        cross_re = (a_re * b_re + a_im * b_im).astype(jnp.bfloat16)
        cross_im = (a_im * b_re - a_re * b_im).astype(jnp.bfloat16)
        from_re = dot(cross_re, table[WRE_ROW : WRE_ROW + 256])
        from_im = dot(cross_im, table[WIM_ROW : WIM_ROW + 256])
        u_re, v_re = from_re[:, :LANES], from_re[:, LANES:]
        u_im, v_im = from_im[:, :LANES], from_im[:, LANES:]
        back_u = jnp.concatenate([u_re - u_im, u_re + u_im], axis=1).astype(jnp.bfloat16)
        back_v = jnp.concatenate([v_im + v_re, v_im - v_re], axis=1).astype(jnp.bfloat16)
        scores = dot(
            table[BACK_ROW : BACK_ROW + SIDE, : 2 * BAND],
            jnp.concatenate([back_u, back_v], axis=0),
        )
        largest = jnp.max(scores, axis=0, keepdims=True)
        weights = jnp.exp2((scores - largest) * EXP2_SCALE).astype(jnp.bfloat16)
        labels = wrapped(shift_rows, centre_row)
        labels = jnp.where(kind == 0, 1.0, jnp.where(kind == 1, labels, 0.0)).astype(jnp.bfloat16)
        sums = dot(labels, weights)
        peak[pl.ds(pair, 1), :] = largest
        total[pl.ds(pair, 1), :] = sums[0:1]
        moment[pl.ds(pair, 1), :] = sums[1:2]
        centre[pl.ds(pair, 1), :] = jnp.broadcast_to(centre_col, (1, 256))

    def displacements(first, count):
        wide = iota((count, 256), 1)
        near = wide < LANES
        shift = jnp.where(near, wide, SIDE + LANES - wide)
        valid = (near & (wide <= HALF)) | ((wide > LANES) & (wide < LANES + HALF))
        height = jnp.where(valid, peak[first : first + count], -jnp.inf)
        top = jnp.max(height, axis=1, keepdims=True)
        share = jnp.exp2((height - top) * EXP2_SCALE)
        share = jnp.where(valid, share, 0.0)
        mass = share * total[first : first + count]
        whole = jnp.sum(mass, axis=1, keepdims=True)
        labels = wrapped(shift, centre[first : first + count])
        scale = 1.0 / (whole * PIXEL_UNIT)
        rows = jnp.sum(share * moment[first : first + count], axis=1, keepdims=True) * scale
        cols = jnp.sum(mass * labels, axis=1, keepdims=True) * scale
        return rows, cols

    mesh_lane = iota((16, LANES), 1)
    mesh_row = iota((16, LANES), 0)
    mesh_peers = (
        (has_right, has_left, (sec, tile + 1)),
        (has_left, has_right, (sec, tile - 1)),
        (has_below, has_above, (sec, tile + GRID_COLS)),
        (has_above, has_below, (sec, tile - GRID_COLS)),
    )
    mesh_copies = [
        pltpu.make_async_remote_copy(
            src_ref=mesh_own,
            dst_ref=mesh_in.at[i],
            send_sem=mesh_send.at[i],
            recv_sem=mesh_recv.at[i],
            device_id=device,
            device_id_type=MESH,
        )
        for i, (_, _, device) in enumerate(mesh_peers)
    ]

    def send_mesh():
        rows, cols = displacements(0, 16)
        held = jnp.where(mesh_row < SLOTS, counts[0, 0], counts[0, sections - 1])
        last = jnp.where(has_after, 2 * SLOTS, SLOTS)
        usable = ((mesh_row & (SLOTS - 1)) < held) & (mesh_row < last)
        values = jnp.where(mesh_lane == 0, rows, jnp.where(mesh_lane == 1, cols, 1.0))
        mesh_own[...] = jnp.where(usable & (mesh_lane < 3), values, 0.0)
        for copy, (there, _, _) in zip(mesh_copies, mesh_peers):

            @pl.when(there)
            def _(copy=copy):
                copy.start()

    def smooth():
        for i, (copy, (_, comes, _)) in enumerate(zip(mesh_copies, mesh_peers)):

            @pl.when(comes)
            def _(copy=copy):
                copy.wait_recv()

            @pl.when(jnp.logical_not(comes))
            def _(i=i):
                mesh_in[i] = jnp.zeros((16, LANES), jnp.float32)

        beside = []
        for k in range(sections):
            for r in range(PATCH_ROWS):
                for c in range(PATCH_COLS):
                    base = SLOTS * k

                    def at(ref, row, col, base=base):
                        q = base + PATCH_COLS * row + col
                        return ref[q : q + 1]

                    own = mesh_own
                    parts = [
                        at(own, r, c - 1) if c > 0 else at(mesh_in.at[0], r, PATCH_COLS - 1),
                        at(own, r, c + 1) if c < PATCH_COLS - 1 else at(mesh_in.at[1], r, 0),
                        at(own, r - 1, c) if r > 0 else at(mesh_in.at[2], PATCH_ROWS - 1, c),
                        at(own, r + 1, c) if r < PATCH_ROWS - 1 else at(mesh_in.at[3], 0, c),
                    ]
                    beside.append(functools.reduce(jnp.add, parts))
        beside = jnp.concatenate(beside, axis=0)
        own = mesh_own[...]
        value = own[:, 2:3] * (2.0 * own + beside) / (2.0 + beside[:, 2:3])
        for k in range(sections):
            for axis in range(2):
                diagonal = jnp.where(mesh_row == mesh_lane + SLOTS * k, value[:, axis : axis + 1], 0.0)
                flow_out[k, 0, axis : axis + 1, :] = jnp.sum(diagonal, axis=0, keepdims=True)[:, :SLOTS]

    def finish_seams():
        rows, cols = displacements(16, 16)
        row, where = iota((16, LANES), 0), iota((16, LANES), 1)
        usable = ((row < 4) & has_right) | ((row >= 4) & has_below)
        for k in range(sections):
            pick = jnp.where(where < PATCH_ROWS, 2 * k + where, 4 + 4 * k + where - PATCH_ROWS)
            pick = (row == pick) & usable
            for axis, value in enumerate((rows, cols)):
                seam = jnp.sum(jnp.where(pick, value, 0.0), axis=0, keepdims=True)
                seams_out[k, 0, axis : axis + 1, :] = seam[:, :EDGES]

    def own_spectra(group, carry):
        spectra(group)
        return carry

    lax.fori_loop(0, 2, own_spectra, 0)

    def stage(i, carry):
        @pl.when((i == 2) & has_after)
        def _():
            next_rem[0].wait_recv()
            next_main[0].wait_recv()

        @pl.when((i == 3) & has_after)
        def _():
            next_rem[1].wait_recv()
            next_main[1].wait_recv()

        @pl.when(i == 4)
        def _():
            send_mesh()

        @pl.when((i == 4) & has_right)
        def _():
            left_rem.wait_recv()
            for copy in left_main:
                copy.wait_recv()

        @pl.when((i == 5) & has_below)
        def _():
            below_rem[0].wait_recv()
            for copy in below_main[0]:
                copy.wait_recv()

        @pl.when(i == 6)
        def _():
            smooth()

        @pl.when((i == 6) & has_below)
        def _():
            below_rem[1].wait_recv()
            for copy in below_main[1]:
                copy.wait_recv()

        there = (
            (i < 2)
            | ((i < 4) & has_after)
            | ((i == 4) & has_right)
            | ((i > 4) & has_below)
        )

        @pl.when(there)
        def _():
            spectra(i + 2)
            for p in range(GROUP):
                pair = GROUP * i + p
                cross = i < 4
                left_source = SLOTS * (p // 2) + PATCH_COLS * (p % 2) + PATCH_COLS - 1
                below_source = SLOTS * (i - 5) + PATCH_COLS + p
                source = jnp.where(cross, pair, jnp.where(i == 4, left_source, below_source))
                section = jnp.where(cross, i // 2, 0)
                slot = jnp.where(cross, lax.rem(i, 2) * GROUP + p, 0)
                centre_row = jnp.where(cross, offsets[section, 0, 0, slot], 0)
                centre_col = jnp.where(cross, offsets[section, 0, 1, slot], 0)
                displace(pair, source, SLOTS + pair, centre_row, centre_col)

        return carry

    lax.fori_loop(0, 7, stage, 0)
    finish_seams()

    def drain(copies):
        for copy in copies:
            copy.wait_send()

    @pl.when(has_above)
    def _():
        drain(below_rem + below_main[0] + below_main[1])

    @pl.when(has_left)
    def _():
        drain([left_rem] + left_main)

    @pl.when(has_before)
    def _():
        drain(next_main + next_rem)

    for copy, (there, _, _) in zip(mesh_copies, mesh_peers):

        @pl.when(there)
        def _(copy=copy):
            copy.wait_send()


def local(patches, margins, offsets, counts):
    sections = patches.shape[0]
    hbm = pl.BlockSpec(memory_space=pltpu.HBM)
    smem = pl.BlockSpec(memory_space=pltpu.SMEM)
    vmem = pl.BlockSpec(memory_space=pltpu.VMEM)
    bf16, f32 = jnp.bfloat16, jnp.float32
    return tuple(
        pl.pallas_call(
            functools.partial(kernel, sections),
            out_shape=(
                jax.ShapeDtypeStruct((sections, 1, 2, SLOTS), f32),
                jax.ShapeDtypeStruct((sections, 1, 2, EDGES), f32),
            ),
            in_specs=[hbm, hbm, hbm, smem, smem],
            out_specs=(vmem, vmem),
            scratch_shapes=[
                pltpu.VMEM((TABLE_ROWS, 256), bf16),
                pltpu.VMEM((IMAGES, SIDE, LANES), bf16),
                pltpu.VMEM((12, SIDE, LANES), bf16),
                pltpu.VMEM((28, SIDE, TAIL), bf16),
                pltpu.VMEM((IMAGES, 2, BAND, 256), bf16),
                pltpu.VMEM((PAIR_ROWS, 256), f32),
                pltpu.VMEM((PAIR_ROWS, 256), f32),
                pltpu.VMEM((PAIR_ROWS, 256), f32),
                pltpu.VMEM((PAIR_ROWS, 256), jnp.int32),
                pltpu.VMEM((16, LANES), f32),
                pltpu.VMEM((4, 16, LANES), f32),
                pltpu.SemaphoreType.DMA((8,)),
                pltpu.SemaphoreType.DMA((19,)),
                pltpu.SemaphoreType.DMA((19,)),
                pltpu.SemaphoreType.DMA((4,)),
                pltpu.SemaphoreType.DMA((4,)),
            ],
            compiler_params=pltpu.CompilerParams(
                collective_id=0, has_side_effects=True, vmem_limit_bytes=60 * 1024 * 1024
            ),
        )(patches, margins, jnp.asarray(tables()), jnp.swapaxes(offsets, 2, 3), jnp.swapaxes(counts, 0, 1))
    )


def solution(mesh):
    return jax.shard_map(
        local,
        mesh=mesh,
        in_specs=(
            P("sec", "xy", None, None, None),
            P("sec", "xy", None, None, None),
            P("sec", "xy", None, None),
            P("sec", "xy"),
        ),
        out_specs=(P("sec", "xy", None, None), P("sec", "xy", None, None)),
        check_vma=False,
    )
```

profile of v0, /device:TPU:42, one launch (start us, length us, event | category | flops | bytes accessed | tf_op | source)
XLA Modules:
  0.0 47.8 jit_solution(13159851397215465834)
XLA Ops:
  0.6 44.7 %shard_map.68 = (f32[2,1,2,8]{3,2,1,0:T(2,128)}, f32[2,1,2,6]{3,2,1,0:T(2,128)}) custom-call(bf16[2,1,8,160,160]{4,3,2,1,0:T(8,128)(2,1)} %patches.1, bf16[2,1,6,160,160]{4,3,2,1,0:T(8,128)(2,1)} %margins.1, bf16[1888,256]{1,0:T(8,128)(2,1)} %constant.2.clone.table_in, s32[2,1,2,8]{3,2,1,0:T(2,128)} %bitcast.2, s32[1,2]{1,0:T(1,128)} %bitcast.3), custom_call_target="tpu_custom_call" | custom-call | tf_op jit(solution)/shard_map/pallas_call | solution.py:519
  45.4 1.2 %copy.9 = f32[2,1,2,8]{3,2,1,0:T(2,128)} copy(f32[2,1,2,8]{3,2,1,0:T(2,128)} %get-tuple-element.4) | data formatting | bytes 256
  46.6 1.2 %copy.10 = f32[2,1,2,6]{3,2,1,0:T(2,128)} copy(f32[2,1,2,6]{3,2,1,0:T(2,128)} %get-tuple-element.5) | data formatting | bytes 192
where the time goes:
time: 48.1 us; the launch traced here: 47.8 us
  Pallas kernels  44.7 us (93%)
  local copies, waits for them, and re-layouts  2.48 us (5%)
  between operations  0.64 us (1%)
    pallas_call x1, Pallas kernels, local(): pl.pallas_call(functools.partial(kernel, sections), out_shape=(jax.ShapeD...  44.7 us
    unnamed x2, local copies, waits for them, and re-layouts  2.48 us

commit v1 on v0

--- a/solution.py
+++ b/solution.py
@@ -26,7 +26,7 @@
 EXP2_SCALE = SCORE_SCALE * LOG2E
 
 T_ROW = 0
-WRE_ROW = T_ROW + GROUP * 256
+WRE_ROW = T_ROW + 256
 WIM_ROW = WRE_ROW + 256
 CS_ROW = WIM_ROW + 256
 BACK_ROW = CS_ROW + 2 * BAND
@@ -53,11 +53,7 @@
     right = np.zeros((SIDE, 256), np.float32)
     right[:, :n] = cosine[:, :n]
     right[:, 128 : 128 + n] = sine[:, :n]
-    for p in range(GROUP):
-        base = T_ROW + 256 * p
-        out[base : base + LANES] = right[:LANES]
-        low = base + LANES + TAIL * p
-        out[low : low + TAIL] = right[LANES:]
+    out[T_ROW : T_ROW + SIDE] = right
     inner = np.ones((n, 1), np.float32)
     inner[0] = inner[HALF] = 0.0
     cos_half, sin_half = cosine[:n, :n], sine[:n, :n]
@@ -94,10 +90,12 @@
     patches,
     margins,
     table_in,
+    offsets_in,
+    counts_in,
+    flow_out,
+    seams_out,
     offsets,
     counts,
-    flow_out,
-    seams_out,
     table,
     main,
     rem,
@@ -114,6 +112,7 @@
     recv_sem,
     mesh_send,
     mesh_recv,
+    ready,
 ):
     sec = lax.axis_index("sec")
     tile = lax.axis_index("xy")
@@ -126,6 +125,34 @@
     has_right = column < GRID_COLS - 1
     has_above = tile >= GRID_COLS
     has_below = tile < tile_total - GRID_COLS
+    place = lax.rem(tile, 2 * GRID_COLS)
+    host = place >= GRID_COLS
+    guest = jnp.logical_not(host)
+    first_turn = (place & 2) == 0
+    second_turn = jnp.logical_not(first_turn)
+
+    barrier = pltpu.get_barrier_semaphore()
+    beside = (
+        (has_before, (sec - 1, tile)),
+        (has_after, (sec + 1, tile)),
+        (has_left, (sec, tile - 1)),
+        (has_right, (sec, tile + 1)),
+    )
+    across = (
+        (has_above, (sec, tile - GRID_COLS), 1),
+        (has_below, (sec, tile + GRID_COLS), 0),
+    )
+    for there, device in beside:
+
+        @pl.when(there)
+        def _(device=device):
+            pl.semaphore_signal(barrier, inc=1, device_id=device, device_id_type=MESH)
+
+    for there, device, _ in across:
+
+        @pl.when(there & guest)
+        def _(device=device):
+            pl.semaphore_signal(barrier, inc=1, device_id=device, device_id_type=MESH)
 
     local_copies = []
 
@@ -139,7 +166,6 @@
         fetch(margins.at[k, 0, :, :, pl.ds(LANES, TAIL)], raw.at[pl.ds(16 + EDGES * k, EDGES)])
         for k in range(sections)
     ]
-    table_copy = fetch(table_in, table)
     patch_raw = [
         fetch(patches.at[k, 0, :, :, pl.ds(LANES, TAIL)], raw.at[pl.ds(SLOTS * k, SLOTS)])
         for k in range(sections)
@@ -148,21 +174,7 @@
         fetch(patches.at[k, 0, :, :, pl.ds(0, LANES)], main.at[pl.ds(SLOTS * k, SLOTS)])
         for k in range(sections)
     ]
-
-    barrier = pltpu.get_barrier_semaphore()
-    peers = (
-        (has_before, (sec - 1, tile)),
-        (has_after, (sec + 1, tile)),
-        (has_left, (sec, tile - 1)),
-        (has_right, (sec, tile + 1)),
-        (has_above, (sec, tile - GRID_COLS)),
-        (has_below, (sec, tile + GRID_COLS)),
-    )
-    for there, device in peers:
-
-        @pl.when(there)
-        def _(device=device):
-            pl.semaphore_signal(barrier, inc=1, device_id=device, device_id_type=MESH)
+    rest = [fetch(table_in, table), fetch(offsets_in, offsets), fetch(counts_in, counts)]
 
     def transfer(number, src, dst, device):
         return pltpu.make_async_remote_copy(
@@ -217,27 +229,40 @@
     def pack(slot, sources):
         rem[slot] = jnp.concatenate([raw[i] for i in sources], axis=1)
 
-    table_copy.wait()
+    greeted = functools.reduce(jnp.add, [there.astype(jnp.int32) for there, _ in beside])
+    greeted += functools.reduce(jnp.add, [(there & host).astype(jnp.int32) for there, _, _ in across])
+    pl.semaphore_wait(barrier, greeted)
+    for there, device, side in across:
+
+        @pl.when(there & host)
+        def _(device=device, side=side):
+            pl.semaphore_signal(ready.at[side], inc=1, device_id=device, device_id_type=MESH)
+
+    @pl.when(has_left)
+    def _():
+        start(left_main)
+
+    @pl.when(has_above & host & first_turn)
+    def _():
+        start(below_main[0])
+
+    @pl.when(has_before)
+    def _():
+        start(next_main)
+
     for copy in margin_raw:
         copy.wait()
+    pack(9, [16, 17, 16 + EDGES, 16 + EDGES + 1])
     pack(10, [16 + PATCH_ROWS + c for c in range(4)])
     pack(11, [16 + EDGES + PATCH_ROWS + c for c in range(4)])
-    pack(9, [16, 17, 16 + EDGES, 16 + EDGES + 1])
-
-    greeted = functools.reduce(jnp.add, [there.astype(jnp.int32) for there, _ in peers])
-    pl.semaphore_wait(barrier, greeted)
-
-    @pl.when(has_above)
-    def _():
-        start(below_rem + below_main[0] + below_main[1])
 
     @pl.when(has_left)
     def _():
-        start([left_rem] + left_main)
-
-    @pl.when(has_before)
-    def _():
-        start(next_main)
+        start([left_rem])
+
+    @pl.when(has_above & host & first_turn)
+    def _():
+        start([below_rem[0], below_rem[1]] + below_main[1])
 
     for copy in patch_raw:
         copy.wait()
@@ -248,8 +273,11 @@
     def _():
         start(next_rem)
 
-    for copy in patch_main:
+    for copy in patch_main + rest:
         copy.wait()
+
+    def start_below():
+        start([below_rem[0]] + below_main[0] + [below_rem[1]] + below_main[1])
 
     lane = iota((1, LANES), 1)
     group_of_lane = lane // TAIL
@@ -278,45 +306,51 @@
             sums = sums + jnp.where(group_of_lane == p, tail_sum, 0.0)
             variance = jnp.sum(sums, axis=1, keepdims=True) * (1.0 / (SIDE * SIDE))
             scales.append(1.0 / jnp.sqrt(variance + 1e-05))
-        tail = (tail * by_lane(scales)).astype(jnp.bfloat16)
+        tail = tail * by_lane(scales)
+        normal = []
+        for p in range(GROUP):
+            head = (main[GROUP * group + p].astype(jnp.float32) - means[p]) * scales[p]
+            rolled = tail if p == 0 else pltpu.roll(tail, LANES - TAIL * p, 1)
+            normal.append(jnp.concatenate([head, rolled], axis=1).astype(jnp.bfloat16))
+        normal = jnp.concatenate(normal, axis=0)
+        rows = dot(normal, table[T_ROW : T_ROW + 256]).astype(jnp.bfloat16)
         for p in range(GROUP):
             image = GROUP * group + p
-            head = ((main[image].astype(jnp.float32) - means[p]) * scales[p]).astype(jnp.bfloat16)
-            normal = jnp.concatenate([head, tail], axis=1)
-            rows = dot(normal, table[T_ROW + 256 * p : T_ROW + 256 * (p + 1)]).astype(jnp.bfloat16)
-            both = dot(table[CS_ROW : CS_ROW + 2 * BAND, :SIDE], rows)
+            both = dot(table[CS_ROW : CS_ROW + 2 * BAND, :SIDE], rows[SIDE * p : SIDE * (p + 1)])
             cc, cs = both[:BAND, :LANES], both[:BAND, LANES:]
             sc, ss = both[BAND:, :LANES], both[BAND:, LANES:]
             spec[image, 0] = jnp.concatenate([cc - ss, cc + ss], axis=1).astype(jnp.bfloat16)
             spec[image, 1] = jnp.concatenate([-(sc + cs), sc - cs], axis=1).astype(jnp.bfloat16)
 
-    shift_rows = iota((16, SIDE), 1)
-    kind = iota((16, SIDE), 0)
-
-    def displace(pair, source, target, centre_row, centre_col):
-        a_re, a_im = spec[source, 0].astype(jnp.float32), spec[source, 1].astype(jnp.float32)
-        b_re, b_im = spec[target, 0].astype(jnp.float32), spec[target, 1].astype(jnp.float32)
-        cross_re = (a_re * b_re + a_im * b_im).astype(jnp.bfloat16)
-        cross_im = (a_im * b_re - a_re * b_im).astype(jnp.bfloat16)
-        from_re = dot(cross_re, table[WRE_ROW : WRE_ROW + 256])
-        from_im = dot(cross_im, table[WIM_ROW : WIM_ROW + 256])
-        u_re, v_re = from_re[:, :LANES], from_re[:, LANES:]
-        u_im, v_im = from_im[:, :LANES], from_im[:, LANES:]
-        back_u = jnp.concatenate([u_re - u_im, u_re + u_im], axis=1).astype(jnp.bfloat16)
-        back_v = jnp.concatenate([v_im + v_re, v_im - v_re], axis=1).astype(jnp.bfloat16)
-        scores = dot(
-            table[BACK_ROW : BACK_ROW + SIDE, : 2 * BAND],
-            jnp.concatenate([back_u, back_v], axis=0),
-        )
-        largest = jnp.max(scores, axis=0, keepdims=True)
-        weights = jnp.exp2((scores - largest) * EXP2_SCALE).astype(jnp.bfloat16)
-        labels = wrapped(shift_rows, centre_row)
-        labels = jnp.where(kind == 0, 1.0, jnp.where(kind == 1, labels, 0.0)).astype(jnp.bfloat16)
-        sums = dot(labels, weights)
-        peak[pl.ds(pair, 1), :] = largest
-        total[pl.ds(pair, 1), :] = sums[0:1]
-        moment[pl.ds(pair, 1), :] = sums[1:2]
-        centre[pl.ds(pair, 1), :] = jnp.broadcast_to(centre_col, (1, 256))
+    shift_rows = iota((SIDE, LANES), 0)
+
+    def displace(items):
+        cross_re, cross_im = [], []
+        for _, source, target, _, _ in items:
+            a_re, a_im = spec[source, 0].astype(jnp.float32), spec[source, 1].astype(jnp.float32)
+            b_re, b_im = spec[target, 0].astype(jnp.float32), spec[target, 1].astype(jnp.float32)
+            cross_re.append((a_re * b_re + a_im * b_im).astype(jnp.bfloat16))
+            cross_im.append((a_im * b_re - a_re * b_im).astype(jnp.bfloat16))
+        all_re = dot(jnp.concatenate(cross_re, axis=0), table[WRE_ROW : WRE_ROW + 256])
+        all_im = dot(jnp.concatenate(cross_im, axis=0), table[WIM_ROW : WIM_ROW + 256])
+        for p, (pair, _, _, centre_row, centre_col) in enumerate(items):
+            from_re, from_im = all_re[BAND * p : BAND * (p + 1)], all_im[BAND * p : BAND * (p + 1)]
+            u_re, v_re = from_re[:, :LANES], from_re[:, LANES:]
+            u_im, v_im = from_im[:, :LANES], from_im[:, LANES:]
+            back_u = jnp.concatenate([u_re - u_im, u_re + u_im], axis=1).astype(jnp.bfloat16)
+            back_v = jnp.concatenate([v_im + v_re, v_im - v_re], axis=1).astype(jnp.bfloat16)
+            scores = dot(
+                table[BACK_ROW : BACK_ROW + SIDE, : 2 * BAND],
+                jnp.concatenate([back_u, back_v], axis=0),
+            )
+            largest = jnp.max(scores, axis=0, keepdims=True)
+            weights = jnp.exp2((scores - largest) * EXP2_SCALE)
+            labels = wrapped(shift_rows, centre_row)
+            labels = jnp.concatenate([labels, labels], axis=1)
+            peak[pl.ds(pair, 1), :] = largest
+            total[pl.ds(pair, 1), :] = jnp.sum(weights, axis=0, keepdims=True)
+            moment[pl.ds(pair, 1), :] = jnp.sum(weights * labels, axis=0, keepdims=True)
+            centre[pl.ds(pair, 1), :] = jnp.broadcast_to(centre_col, (1, 256))
 
     def displacements(first, count):
         wide = iota((count, 256), 1)
@@ -423,6 +457,28 @@
     lax.fori_loop(0, 2, own_spectra, 0)
 
     def stage(i, carry):
+        for there, _, side in across:
+
+            @pl.when((i == 1) & there & guest)
+            def _(side=side):
+                pl.semaphore_wait(ready.at[1 - side], 1)
+
+        @pl.when((i == 1) & has_above & guest & first_turn)
+        def _():
+            start_below()
+
+        @pl.when((i == 2) & has_above & host & second_turn)
+        def _():
+            start_below()
+
+        @pl.when((i == 4) & has_above & guest & second_turn)
+        def _():
+            start_below()
+
+        @pl.when((i == 5) & has_below)
+        def _():
+            below_rem[0].wait_recv()
+
         @pl.when((i == 2) & has_after)
         def _():
             next_rem[0].wait_recv()
@@ -445,7 +501,6 @@
 
         @pl.when((i == 5) & has_below)
         def _():
-            below_rem[0].wait_recv()
             for copy in below_main[0]:
                 copy.wait_recv()
 
@@ -469,6 +524,7 @@
         @pl.when(there)
         def _():
             spectra(i + 2)
+            items = []
             for p in range(GROUP):
                 pair = GROUP * i + p
                 cross = i < 4
@@ -479,7 +535,8 @@
                 slot = jnp.where(cross, lax.rem(i, 2) * GROUP + p, 0)
                 centre_row = jnp.where(cross, offsets[section, 0, 0, slot], 0)
                 centre_col = jnp.where(cross, offsets[section, 0, 1, slot], 0)
-                displace(pair, source, SLOTS + pair, centre_row, centre_col)
+                items.append((pair, source, SLOTS + pair, centre_row, centre_col))
+            displace(items)
 
         return carry
 
@@ -512,19 +569,20 @@
 def local(patches, margins, offsets, counts):
     sections = patches.shape[0]
     hbm = pl.BlockSpec(memory_space=pltpu.HBM)
-    smem = pl.BlockSpec(memory_space=pltpu.SMEM)
     vmem = pl.BlockSpec(memory_space=pltpu.VMEM)
     bf16, f32 = jnp.bfloat16, jnp.float32
-    return tuple(
+    flow, seams = (
         pl.pallas_call(
             functools.partial(kernel, sections),
             out_shape=(
                 jax.ShapeDtypeStruct((sections, 1, 2, SLOTS), f32),
                 jax.ShapeDtypeStruct((sections, 1, 2, EDGES), f32),
             ),
-            in_specs=[hbm, hbm, hbm, smem, smem],
+            in_specs=[hbm] * 5,
             out_specs=(vmem, vmem),
             scratch_shapes=[
+                pltpu.SMEM((sections, 1, 2, SLOTS), jnp.int32),
+                pltpu.SMEM((1, sections), jnp.int32),
                 pltpu.VMEM((TABLE_ROWS, 256), bf16),
                 pltpu.VMEM((IMAGES, SIDE, LANES), bf16),
                 pltpu.VMEM((12, SIDE, LANES), bf16),
@@ -536,17 +594,34 @@
                 pltpu.VMEM((PAIR_ROWS, 256), jnp.int32),
                 pltpu.VMEM((16, LANES), f32),
                 pltpu.VMEM((4, 16, LANES), f32),
-                pltpu.SemaphoreType.DMA((8,)),
+                pltpu.SemaphoreType.DMA((9,)),
                 pltpu.SemaphoreType.DMA((19,)),
                 pltpu.SemaphoreType.DMA((19,)),
                 pltpu.SemaphoreType.DMA((4,)),
                 pltpu.SemaphoreType.DMA((4,)),
+                pltpu.SemaphoreType.REGULAR((2,)),
             ],
             compiler_params=pltpu.CompilerParams(
                 collective_id=0, has_side_effects=True, vmem_limit_bytes=60 * 1024 * 1024
             ),
         )(patches, margins, jnp.asarray(tables()), jnp.swapaxes(offsets, 2, 3), jnp.swapaxes(counts, 0, 1))
     )
+    return tuple(
+        pl.pallas_call(
+            hand_over,
+            out_shape=(
+                jax.ShapeDtypeStruct(flow.shape, f32),
+                jax.ShapeDtypeStruct(seams.shape, f32),
+            ),
+            in_specs=[vmem, vmem],
+            out_specs=(vmem, vmem),
+        )(flow, seams)
+    )
+
+
+def hand_over(flow_in, seams_in, flow_out, seams_out):
+    flow_out[...] = flow_in[...]
+    seams_out[...] = seams_in[...]
 
 
 def solution(mesh):

time: 48.1 us -> 39.3 us (0.82)
  the two profiles are of different devices: /device:TPU:42 before, /device:TPU:122 now
where the time goes in v1:
time: 39.3 us; the launch traced here: 39.1 us
  Pallas kernels  38.4 us (98%)
  between operations  0.64 us (2%)
    pallas_call x1, Pallas kernels, local(): pl.pallas_call(functools.partial(kernel, sections), out_shape=(jax.ShapeD...  37.2 us
    pallas_call x1, Pallas kernels, local(): pl.pallas_call(hand_over, out_shape=(jax.ShapeDtypeStruct(flow.shape, f32...  1.26 us

profile of v1, /device:TPU:122, one launch (start us, length us, event | category | flops | bytes accessed | tf_op | source)
XLA Modules:
  0.0 39.1 jit_solution(12707126289924613562)
XLA Ops:
  0.6 37.2 %shard_map.68 = (f32[2,1,2,8]{3,2,1,0:T(2,128)}, f32[2,1,2,6]{3,2,1,0:T(2,128)}) custom-call(bf16[2,1,8,160,160]{4,3,2,1,0:T(8,128)(2,1)} %patches.1, bf16[2,1,6,160,160]{4,3,2,1,0:T(8,128)(2,1)} %margins.1, bf16[1120,256]{1,0:T(8,128)(2,1)} %constant.2.clone.table_in, s32[2,1,2,8]{3,2,1,0:T(2,128)} %bitcast.2, s32[1,2]{1,0:T(1,128)} %bitcast.3), custom_call_target="tpu_custom_call" | custom-call | tf_op jit(solution)/shard_map/pallas_call | solution.py:575
  37.8 1.3 %shard_map.69 = (f32[2,1,2,8]{3,2,1,0:T(2,128)}, f32[2,1,2,6]{3,2,1,0:T(2,128)}) custom-call(f32[2,1,2,8]{3,2,1,0:T(2,128)} %get-tuple-element.4.flow_in, f32[2,1,2,6]{3,2,1,0:T(2,128)} %get-tuple-element.5.seams_in), custom_call_target="tpu_custom_call" | custom-call | tf_op jit(solution)/shard_map/pallas_call | solution.py:610

commit v2 on v1

--- a/solution.py
+++ b/solution.py
@@ -128,8 +128,10 @@
     place = lax.rem(tile, 2 * GRID_COLS)
     host = place >= GRID_COLS
     guest = jnp.logical_not(host)
-    first_turn = (place & 2) == 0
-    second_turn = jnp.logical_not(first_turn)
+    turns = (
+        jnp.where(place == 0, 1, jnp.where(place == 1, 1, jnp.where(place == 2, 4, jnp.where(place == 3, 4, jnp.where(place == 4, -1, jnp.where(place == 5, -1, jnp.where(place == 6, 2, 2))))))),
+        jnp.where(place == 0, 2, jnp.where(place == 1, 2, jnp.where(place == 2, 5, jnp.where(place == 3, 5, jnp.where(place == 4, -1, jnp.where(place == 5, -1, jnp.where(place == 6, 3, 3))))))),
+    )
 
     barrier = pltpu.get_barrier_semaphore()
     beside = (
@@ -153,28 +155,6 @@
         @pl.when(there & guest)
         def _(device=device):
             pl.semaphore_signal(barrier, inc=1, device_id=device, device_id_type=MESH)
-
-    local_copies = []
-
-    def fetch(src, dst):
-        copy = pltpu.make_async_copy(src, dst, local_sem.at[len(local_copies)])
-        copy.start()
-        local_copies.append(copy)
-        return copy
-
-    margin_raw = [
-        fetch(margins.at[k, 0, :, :, pl.ds(LANES, TAIL)], raw.at[pl.ds(16 + EDGES * k, EDGES)])
-        for k in range(sections)
-    ]
-    patch_raw = [
-        fetch(patches.at[k, 0, :, :, pl.ds(LANES, TAIL)], raw.at[pl.ds(SLOTS * k, SLOTS)])
-        for k in range(sections)
-    ]
-    patch_main = [
-        fetch(patches.at[k, 0, :, :, pl.ds(0, LANES)], main.at[pl.ds(SLOTS * k, SLOTS)])
-        for k in range(sections)
-    ]
-    rest = [fetch(table_in, table), fetch(offsets_in, offsets), fetch(counts_in, counts)]
 
     def transfer(number, src, dst, device):
         return pltpu.make_async_remote_copy(
@@ -238,31 +218,58 @@
         def _(device=device, side=side):
             pl.semaphore_signal(ready.at[side], inc=1, device_id=device, device_id_type=MESH)
 
-    @pl.when(has_left)
+    @pl.when(has_above & (turns[0] < 0))
+    def _():
+        start(below_main[0])
+
+    @pl.when(has_left & guest)
     def _():
         start(left_main)
 
-    @pl.when(has_above & host & first_turn)
-    def _():
-        start(below_main[0])
-
     @pl.when(has_before)
     def _():
         start(next_main)
+
+    local_copies = []
+
+    def fetch(src, dst):
+        copy = pltpu.make_async_copy(src, dst, local_sem.at[len(local_copies)])
+        copy.start()
+        local_copies.append(copy)
+        return copy
+
+    margin_raw = [
+        fetch(margins.at[k, 0, :, :, pl.ds(LANES, TAIL)], raw.at[pl.ds(16 + EDGES * k, EDGES)])
+        for k in range(sections)
+    ]
+    patch_raw = [
+        fetch(patches.at[k, 0, :, :, pl.ds(LANES, TAIL)], raw.at[pl.ds(SLOTS * k, SLOTS)])
+        for k in range(sections)
+    ]
+    patch_main = [
+        fetch(patches.at[k, 0, :, :, pl.ds(0, LANES)], main.at[pl.ds(SLOTS * k, SLOTS)])
+        for k in range(sections)
+    ]
+    rest = [fetch(table_in, table), fetch(offsets_in, offsets), fetch(counts_in, counts)]
 
     for copy in margin_raw:
         copy.wait()
-    pack(9, [16, 17, 16 + EDGES, 16 + EDGES + 1])
     pack(10, [16 + PATCH_ROWS + c for c in range(4)])
     pack(11, [16 + EDGES + PATCH_ROWS + c for c in range(4)])
 
-    @pl.when(has_left)
+    @pl.when(has_above & (turns[0] < 0))
+    def _():
+        start([below_rem[0]])
+
+    @pl.when(has_above & (turns[1] < 0))
+    def _():
+        start([below_rem[1]] + below_main[1])
+
+    pack(9, [16, 17, 16 + EDGES, 16 + EDGES + 1])
+
+    @pl.when(has_left & guest)
     def _():
         start([left_rem])
-
-    @pl.when(has_above & host & first_turn)
-    def _():
-        start([below_rem[0], below_rem[1]] + below_main[1])
 
     for copy in patch_raw:
         copy.wait()
@@ -275,9 +282,6 @@
 
     for copy in patch_main + rest:
         copy.wait()
-
-    def start_below():
-        start([below_rem[0]] + below_main[0] + [below_rem[1]] + below_main[1])
 
     lane = iota((1, LANES), 1)
     group_of_lane = lane // TAIL
@@ -456,28 +460,25 @@
 
     lax.fori_loop(0, 2, own_spectra, 0)
 
-    def stage(i, carry):
+    def stage(step, carry):
+        late = jnp.where(step == 6, 4, step + 1)
+        i = jnp.where(host & (step >= 4), late, step)
+
         for there, _, side in across:
 
-            @pl.when((i == 1) & there & guest)
+            @pl.when((step == 1) & there & guest)
             def _(side=side):
                 pl.semaphore_wait(ready.at[1 - side], 1)
 
-        @pl.when((i == 1) & has_above & guest & first_turn)
-        def _():
-            start_below()
-
-        @pl.when((i == 2) & has_above & host & second_turn)
-        def _():
-            start_below()
-
-        @pl.when((i == 4) & has_above & guest & second_turn)
-        def _():
-            start_below()
-
-        @pl.when((i == 5) & has_below)
-        def _():
-            below_rem[0].wait_recv()
+        for k in range(sections):
+
+            @pl.when(has_above & (step == turns[k]))
+            def _(k=k):
+                start([below_rem[k]] + below_main[k])
+
+        @pl.when(has_left & host & (step == 5))
+        def _():
+            start([left_rem] + left_main)
 
         @pl.when((i == 2) & has_after)
         def _():
@@ -489,7 +490,7 @@
             next_rem[1].wait_recv()
             next_main[1].wait_recv()
 
-        @pl.when(i == 4)
+        @pl.when(step == 4)
         def _():
             send_mesh()
 
@@ -501,10 +502,11 @@
 
         @pl.when((i == 5) & has_below)
         def _():
+            below_rem[0].wait_recv()
             for copy in below_main[0]:
                 copy.wait_recv()
 
-        @pl.when(i == 6)
+        @pl.when(step == 6)
         def _():
             smooth()
 

time: 39.3 us -> 38.9 us (0.990)
  the two profiles are of different devices: /device:TPU:122 before, /device:TPU:158 now
where the time goes in v2:
time: 38.9 us; the launch traced here: 38.8 us
  Pallas kernels  38.1 us (98%)
  between operations  0.64 us (2%)
    pallas_call x1, Pallas kernels, local(): pl.pallas_call(functools.partial(kernel, sections), out_shape=(jax.ShapeD...  36.9 us
    pallas_call x1, Pallas kernels, local(): pl.pallas_call(hand_over, out_shape=(jax.ShapeDtypeStruct(flow.shape, f32...  1.26 us

profile of v2, /device:TPU:158, one launch (start us, length us, event | category | flops | bytes accessed | tf_op | source)
XLA Modules:
  0.0 38.8 jit_solution(5383865889124088829)
XLA Ops:
  0.6 36.9 %shard_map.68 = (f32[2,1,2,8]{3,2,1,0:T(2,128)}, f32[2,1,2,6]{3,2,1,0:T(2,128)}) custom-call(bf16[2,1,8,160,160]{4,3,2,1,0:T(8,128)(2,1)} %patches.1, bf16[2,1,6,160,160]{4,3,2,1,0:T(8,128)(2,1)} %margins.1, bf16[1120,256]{1,0:T(8,128)(2,1)} %constant.2.clone.table_in, s32[2,1,2,8]{3,2,1,0:T(2,128)} %bitcast.2, s32[1,2]{1,0:T(1,128)} %bitcast.3), custom_call_target="tpu_custom_call" | custom-call | tf_op jit(solution)/shard_map/pallas_call | solution.py:577
  37.5 1.3 %shard_map.69 = (f32[2,1,2,8]{3,2,1,0:T(2,128)}, f32[2,1,2,6]{3,2,1,0:T(2,128)}) custom-call(f32[2,1,2,8]{3,2,1,0:T(2,128)} %get-tuple-element.4.flow_in, f32[2,1,2,6]{3,2,1,0:T(2,128)} %get-tuple-element.5.seams_in), custom_call_target="tpu_custom_call" | custom-call | tf_op jit(solution)/shard_map/pallas_call | solution.py:612

commit v3 on v2

--- a/solution.py
+++ b/solution.py
@@ -129,8 +129,8 @@
     host = place >= GRID_COLS
     guest = jnp.logical_not(host)
     turns = (
-        jnp.where(place == 0, 1, jnp.where(place == 1, 1, jnp.where(place == 2, 4, jnp.where(place == 3, 4, jnp.where(place == 4, -1, jnp.where(place == 5, -1, jnp.where(place == 6, 2, 2))))))),
-        jnp.where(place == 0, 2, jnp.where(place == 1, 2, jnp.where(place == 2, 5, jnp.where(place == 3, 5, jnp.where(place == 4, -1, jnp.where(place == 5, -1, jnp.where(place == 6, 3, 3))))))),
+        jnp.where(place == 0, 1, jnp.where(place == 1, 1, jnp.where(place == 2, 5, jnp.where(place == 3, 1, jnp.where(place == 4, -1, jnp.where(place == 5, -1, jnp.where(place == 6, 2, -1))))))),
+        jnp.where(place == 0, 2, jnp.where(place == 1, 1, jnp.where(place == 2, 5, jnp.where(place == 3, 1, jnp.where(place == 4, -1, jnp.where(place == 5, -1, jnp.where(place == 6, 3, -1))))))),
     )
 
     barrier = pltpu.get_barrier_semaphore()

time: 38.9 us -> 38.2 us (0.982)
  the two profiles are of different devices: /device:TPU:158 before, /device:TPU:26 now
where the time goes in v3:
time: 38.2 us; the launch traced here: 38.1 us
  Pallas kernels  37.4 us (98%)
  between operations  0.64 us (2%)
    pallas_call x1, Pallas kernels, local(): pl.pallas_call(functools.partial(kernel, sections), out_shape=(jax.ShapeD...  36.2 us
    pallas_call x1, Pallas kernels, local(): pl.pallas_call(hand_over, out_shape=(jax.ShapeDtypeStruct(flow.shape, f32...  1.26 us

profile of v3, /device:TPU:26, one launch (start us, length us, event | category | flops | bytes accessed | tf_op | source)
XLA Modules:
  0.0 38.1 jit_solution(11420810378445812206)
XLA Ops:
  0.6 36.2 %shard_map.68 = (f32[2,1,2,8]{3,2,1,0:T(2,128)}, f32[2,1,2,6]{3,2,1,0:T(2,128)}) custom-call(bf16[2,1,8,160,160]{4,3,2,1,0:T(8,128)(2,1)} %patches.1, bf16[2,1,6,160,160]{4,3,2,1,0:T(8,128)(2,1)} %margins.1, bf16[1120,256]{1,0:T(8,128)(2,1)} %constant.2.clone.table_in, s32[2,1,2,8]{3,2,1,0:T(2,128)} %bitcast.2, s32[1,2]{1,0:T(1,128)} %bitcast.3), custom_call_target="tpu_custom_call" | custom-call | tf_op jit(solution)/shard_map/pallas_call | solution.py:577
  36.8 1.3 %shard_map.69 = (f32[2,1,2,8]{3,2,1,0:T(2,128)}, f32[2,1,2,6]{3,2,1,0:T(2,128)}) custom-call(f32[2,1,2,8]{3,2,1,0:T(2,128)} %get-tuple-element.4.flow_in, f32[2,1,2,6]{3,2,1,0:T(2,128)} %get-tuple-element.5.seams_in), custom_call_target="tpu_custom_call" | custom-call | tf_op jit(solution)/shard_map/pallas_call | solution.py:612
